TPU v7x, 32 devices: a whole 2x2x4 slice. The times are simulated.
32 devices in a mesh: brick: 8 (over z, y), level: 4 (over x, core).
Axes of the slice: x: 2, y: 2, z: 4, core: 2. Of those that a mesh axis runs over, the one named last changes fastest.
Arguments:
- adjoint: float32 [5, 32, 64, 128], P(None, 'level', 'brick'), may hold values from -6 to 6
- source: float32 [5, 32, 64, 128], P(None, 'level', 'brick'), may hold values from -48 to 48
- block: bfloat16 [5, 5, 32, 64, 128], P(None, None, 'level', 'brick'), may hold values from -1 to 13
- precond: bfloat16 [5, 5, 32, 64, 128], P(None, None, 'level', 'brick'), may hold values from -0.01 to 0.14
- couple: float32 [3, 32, 64, 128], P(None, 'level', 'brick'), may hold values from 0.1 to 0.6
- solid: int32 [32, 64, 128], P('level', 'brick'), may hold values 0 or 1
- coarse_owner: int32 [4], replicated, may hold values from 0 to 3, each once
Outputs:
- smoothed: float32 [5, 32, 64, 128], P(None, 'level', 'brick')
- coarse_rhs: float32 [4, 5, 16, 32, 16], P('level', None, None, 'brick')
Inputs may be any that keep to these rules, and one draw needn't show every extreme that they name: `coarse_owner`: each level index owns exactly one block.
All inputs are finite; a program needn't handle non-finite values. No bound on the sum of `solid` on one device may be relied on, other than what follows from the above.
Results may differ from a plain program's by a relative error of at most 0.0003.
Values may be sent and summed in bfloat16 or wider, within the bound.
A program may use at most 64 MiB of HBM per device.

v0:
```python
import functools

import jax
import jax.numpy as jnp
from jax import lax
from jax.experimental import pallas as pl
from jax.experimental.pallas import tpu as pltpu
from jax.sharding import PartitionSpec as P

SWEEPS = 4
RELAX = 0.8
MESH = pl.DeviceIdType.MESH


def kernel(
    bricks, levels, fields, nx, ny, zblock,
    owner, adjoint, source, block, precond, couple, solid,
    smoothed, coarse,
    cells, src, raw_b, raw_p, mat_b, mat_p, cpl, sld, near, part, out_halo, in_halo,
    rows_x, packed, got, got_edge, merged,
    in_sem, out_sem, halo_send, halo_recv, end_send, end_recv,
):
    plane = nx * ny
    nz = cells.shape[1]
    half_x, half_y = nx // 2, ny // 2
    width = half_x + 1
    pad = rows_x.shape[0] // ny
    b, l = lax.axis_index("brick"), lax.axis_index("level")
    has = (l < levels - 1, l > 0, b < bricks - 1, b > 0)
    dest = ((b, l - 1), (b, l + 1), (b - 1, l), (b + 1, l))
    can_send = (has[1], has[0], has[3], has[2])

    loads = [
        pltpu.make_async_copy(a, v, in_sem.at[i])
        for i, (a, v) in enumerate(
            (
                (adjoint, cells), (couple, cpl), (block, raw_b),
                (source, src), (solid, sld), (precond, raw_p),
            )
        )
    ]
    for copy in loads:
        copy.start()

    barrier = pltpu.get_barrier_semaphore()
    for k in range(levels):
        to = lax.rem(l + k, levels)
        if k:
            pl.semaphore_signal(barrier, inc=1, device_id=(b, to), device_id_type=MESH)

        @pl.when(has[3])
        def _():
            pl.semaphore_signal(barrier, inc=1, device_id=(b - 1, to), device_id_type=MESH)

        @pl.when(has[2])
        def _():
            pl.semaphore_signal(barrier, inc=1, device_id=(b + 1, to), device_id_type=MESH)

    for i in range(4):

        @pl.when(jnp.logical_not(has[i]))
        def _():
            for e in range(SWEEPS + 1):
                in_halo[e, i] = jnp.zeros(in_halo.shape[2:], jnp.float32)

    @pl.when(jnp.logical_not(has[3]))
    def _():
        got_edge[...] = jnp.zeros_like(got_edge)

    def halo_copy(e, i):
        return pltpu.make_async_remote_copy(
            src_ref=out_halo.at[e, i],
            dst_ref=in_halo.at[e, i],
            send_sem=halo_send.at[e, i],
            recv_sem=halo_recv.at[e, i],
            device_id=dest[i],
            device_id_type=MESH,
        )

    def send(e):
        for f in range(fields):
            at, to = f * plane, f * nx
            out_halo[e, 2, to : to + nx] = cells[pl.ds(at, nx, stride=ny), :]
            out_halo[e, 3, to : to + nx] = cells[pl.ds(at + ny - 1, nx, stride=ny), :]
            to = f * ny
            out_halo[e, 0, to : to + ny] = cells[at : at + ny]
            out_halo[e, 1, to : to + ny] = cells[at + plane - ny : at + plane]
        for i in (2, 3, 0, 1):

            @pl.when(can_send[i])
            def _():
                halo_copy(e, i).start()

    loads[0].wait()
    neighbours = (levels - 1) + levels * (
        has[3].astype(jnp.int32) + has[2].astype(jnp.int32)
    )
    pl.semaphore_wait(barrier, neighbours)
    send(0)

    loads[1].wait()
    shape = (nx, ny, nz)
    row = lax.broadcasted_iota(jnp.int32, shape, 1).reshape(plane, nz)
    lane = lax.broadcasted_iota(jnp.int32, (plane, nz), 1)
    cy, cz = cpl[plane : 2 * plane], cpl[2 * plane :]
    near[0] = jnp.where(row == ny - 1, 0.0, cy)
    near[1] = jnp.where(row == 0, 0.0, cy)
    near[2] = jnp.where(lane == nz - 1, 0.0, cz)
    near[3] = jnp.where(lane == 0, 0.0, cz)
    loads[2].wait()
    for i in range(fields * fields):
        mat_b[i] = raw_b[i].astype(jnp.float32)
    loads[3].wait()

    def local_part(f):
        at = f * plane
        mid = cells[at : at + plane]
        cube = mid.reshape(shape)
        total = src[at : at + plane]
        for g in range(fields):
            total = total - mat_b[g * fields + f] * cells[g * plane : (g + 1) * plane]
        total = total + near[0] * pltpu.roll(cube, ny - 1, 1).reshape(plane, nz)
        total = total + near[1] * pltpu.roll(cube, 1, 1).reshape(plane, nz)
        total = total + near[2] * pltpu.roll(mid, nz - 1, 1)
        total = total + near[3] * pltpu.roll(mid, 1, 1)
        c = cpl[0:plane]
        part[at : at + ny] = total[:ny] + c[:ny] * mid[ny : 2 * ny]
        part[at + ny : at + plane - ny] = total[ny : plane - ny] + c[ny : plane - ny] * (
            mid[2 * ny :] + mid[: plane - 2 * ny]
        )
        part[at + plane - ny : at + plane] = (
            total[plane - ny :] + c[plane - ny :] * mid[plane - 2 * ny : plane - ny]
        )

    def arrive(e):
        for i in (2, 3, 0, 1):

            @pl.when(has[i])
            def _():
                halo_copy(e, i).wait_recv()

        low_y = cpl[pl.ds(plane, nx, stride=ny), :]
        high_y = cpl[pl.ds(plane + ny - 1, nx, stride=ny), :]
        low_x, high_x = cpl[0:ny], cpl[plane - ny : plane]
        for f in range(fields):
            at = f * plane
            mine = slice(f * ny, (f + 1) * ny)
            part[at + plane - ny : at + plane] += high_x * in_halo[e, 0, mine]
            part[at : at + ny] += low_x * in_halo[e, 1, mine]
            mine = slice(f * nx, (f + 1) * nx)
            spot = pl.ds(at + ny - 1, nx, stride=ny)
            part[spot, :] = part[spot, :] + high_y * in_halo[e, 2, mine]
            spot = pl.ds(at, nx, stride=ny)
            part[spot, :] = part[spot, :] + low_y * in_halo[e, 3, mine]

    for f in range(fields):
        local_part(f)
    loads[4].wait()
    loads[5].wait()
    keep = sld[...] == 0
    for i in range(fields * fields):
        mat_p[i] = jnp.where(keep, RELAX * raw_p[i].astype(jnp.float32), 0.0)

    for sweep in range(SWEEPS):
        if sweep:
            for f in range(fields):
                local_part(f)
        arrive(sweep)
        for f in range(fields):
            at = f * plane
            total = cells[at : at + plane]
            if sweep == 0:
                total = jnp.where(keep, total, 0.0)
            for g in range(fields):
                total = total + mat_p[f * fields + g] * part[g * plane : (g + 1) * plane]
            cells[at : at + plane] = total
        send(sweep + 1)

    store = pltpu.make_async_copy(cells, smoothed, out_sem)
    store.start()
    for f in range(fields):
        local_part(f)
    fine = lax.broadcasted_iota(jnp.int32, (nz, nz), 0)
    column = lax.broadcasted_iota(jnp.int32, (nz, nz), 1)
    target = column // zblock
    start_of = jnp.full((nz, nz), -nz, jnp.int32)
    for k in range(levels):
        start_of = jnp.where(target == owner[k], k * zblock, start_of)
    gap = fine - 2 * (start_of + column % zblock)
    weight = jnp.where(
        gap == 0, 0.5, jnp.where((gap == 1) | (gap == -1), 0.25, 0.0)
    ).astype(jnp.bfloat16)
    rows_x[...] = jnp.zeros_like(rows_x)
    arrive(SWEEPS)

    for f in range(fields):
        res = jnp.where(keep, part[f * plane : (f + 1) * plane], 0.0)
        cut = [res[x * ny : (x + 1) * ny] for x in range(nx)]
        for k in range(width):
            if k == half_x:
                value = 0.25 * cut[nx - 1]
            else:
                value = 0.5 * cut[2 * k] + 0.25 * cut[2 * k + 1]
                if k:
                    value = value + 0.25 * cut[2 * k - 1]
            spot = (f * width + k) * ny
            rows_x[spot : spot + ny] = value
    line = [rows_x[pl.ds(y, pad, stride=ny), :] for y in range(ny)]
    groups = []
    for k in range(half_y):
        value = 0.5 * line[2 * k] + 0.25 * line[2 * k + 1]
        if k:
            value = value + 0.25 * line[2 * k - 1]
        groups.append(value)
    groups.append(0.25 * line[ny - 1])
    stacked = jnp.concatenate(groups, 0)
    high = stacked.astype(jnp.bfloat16)
    low = (stacked - high.astype(jnp.float32)).astype(jnp.bfloat16)
    product = jnp.dot(high, weight, preferred_element_type=jnp.float32) + jnp.dot(
        low, weight, preferred_element_type=jnp.float32
    )
    spot_of = lax.broadcasted_iota(jnp.int32, (pad, nz), 1) // zblock
    for d in range(levels):
        total = jnp.zeros((pad, nz), jnp.float32)
        for k in range(half_y + 1):
            shift = ((k - d) * zblock) % nz
            moved = product[k * pad : (k + 1) * pad]
            if shift:
                moved = pltpu.roll(moved, shift, 1)
            total = jnp.where(spot_of == k, moved, total)
        packed[d] = total

    def end_copy(k, edge):
        to = lax.rem(l + k, levels)
        return pltpu.make_async_remote_copy(
            src_ref=packed.at[to],
            dst_ref=(got_edge if edge else got).at[l],
            send_sem=end_send.at[edge, k],
            recv_sem=end_recv.at[edge, k],
            device_id=(b + edge, to),
            device_id_type=MESH,
        )

    def end_arrival(k, edge):
        origin = lax.rem(l + levels - k, levels)
        return pltpu.make_async_remote_copy(
            src_ref=packed.at[l],
            dst_ref=(got_edge if edge else got).at[origin],
            send_sem=end_send.at[edge, k],
            recv_sem=end_recv.at[edge, k],
            device_id=(b, origin),
            device_id_type=MESH,
        )

    @pl.when(has[2])
    def _():
        for k in range(levels):
            end_copy(k, 1).start()

    for k in range(1, levels):
        end_copy(k, 0).start()
    got[l] = packed[l]
    store.wait()
    for e in range(SWEEPS + 1):
        for i in range(4):

            @pl.when(can_send[i])
            def _():
                halo_copy(e, i).wait_send()

    for k in range(1, levels):
        end_arrival(k, 0).wait_recv()

    @pl.when(has[3])
    def _():
        for k in range(levels):
            end_arrival(k, 1).wait_recv()

    for s in range(levels):
        edge = pltpu.roll(got_edge[s], (-half_y * zblock) % nz, 1)
        merged[s] = got[s] + jnp.where(spot_of == 0, edge, 0.0)
    for f in range(fields):
        for s in range(levels):
            at = f * width
            coarse[f, s * half_x : (s + 1) * half_x] = merged[s, at : at + half_x]
            if s:
                coarse[f, s * half_x : s * half_x + 1] = (
                    merged[s, at : at + 1] + merged[s - 1, at + half_x : at + width]
                )

    for k in range(1, levels):
        end_copy(k, 0).wait_send()

    @pl.when(has[2])
    def _():
        for k in range(levels):
            end_copy(k, 1).wait_send()


def shards(bricks, levels, adjoint, source, block, precond, couple, solid, coarse_owner):
    fields, nx, ny, nz = adjoint.shape
    plane = nx * ny
    zblock = nz // (2 * levels)
    half_x, half_y = nx // 2, ny // 2
    pad = -(-fields * (half_x + 1) // 8) * 8
    flat = fields * plane
    halo = fields * max(nx, ny)
    f32, bf16 = jnp.float32, jnp.bfloat16
    vmem, dma = pltpu.VMEM, pltpu.SemaphoreType.DMA
    anywhere = pl.BlockSpec(memory_space=pl.ANY)
    cells, coarse = pl.pallas_call(
        functools.partial(kernel, bricks, levels, fields, nx, ny, zblock),
        out_shape=(
            jax.ShapeDtypeStruct((flat, nz), f32),
            jax.ShapeDtypeStruct((fields, levels * half_x, nz), f32),
        ),
        in_specs=[pl.BlockSpec(memory_space=pltpu.SMEM)] + [anywhere] * 6,
        out_specs=(anywhere, pl.BlockSpec(memory_space=pltpu.VMEM)),
        scratch_shapes=[
            vmem((flat, nz), f32),
            vmem((flat, nz), f32),
            vmem((fields * fields, plane, nz), bf16),
            vmem((fields * fields, plane, nz), bf16),
            vmem((fields * fields, plane, nz), f32),
            vmem((fields * fields, plane, nz), f32),
            vmem((3 * plane, nz), f32),
            vmem((plane, nz), jnp.int32),
            vmem((4, plane, nz), f32),
            vmem((flat, nz), f32),
            vmem((SWEEPS + 1, 4, halo, nz), f32),
            vmem((SWEEPS + 1, 4, halo, nz), f32),
            vmem((pad * ny, nz), f32),
            vmem((levels, pad, nz), f32),
            vmem((levels, pad, nz), f32),
            vmem((levels, pad, nz), f32),
            vmem((levels, pad, nz), f32),
            dma((6,)),
            dma,
            dma((SWEEPS + 1, 4)),
            dma((SWEEPS + 1, 4)),
            dma((2, levels)),
            dma((2, levels)),
        ],
        compiler_params=pltpu.CompilerParams(
            collective_id=0, has_side_effects=True, vmem_limit_bytes=32 * 1024 * 1024
        ),
    )(
        coarse_owner,
        adjoint.reshape(flat, nz),
        source.reshape(flat, nz),
        block.reshape(fields * fields, plane, nz),
        precond.reshape(fields * fields, plane, nz),
        couple.reshape(3 * plane, nz),
        solid.reshape(plane, nz),
    )
    rhs = coarse[:, :, : half_y * zblock].reshape(
        1, fields, levels * half_x, half_y, zblock
    )
    return cells.reshape(adjoint.shape), rhs


def solution(mesh):
    cells = P(None, "level", "brick", None)
    blocks = P(None, None, "level", "brick", None)
    return jax.shard_map(
        functools.partial(shards, mesh.shape["brick"], mesh.shape["level"]),
        mesh=mesh,
        in_specs=(cells, cells, blocks, blocks, cells, P("level", "brick", None), P()),
        out_specs=(cells, P("level", None, None, "brick", None)),
        check_vma=False,
    )
```

profile of v0, /device:TPU:0, one launch (start us, length us, event | category | flops | bytes accessed | tf_op | source)
XLA Modules:
  0.0 34.3 jit_solution(8838681584164186362)
XLA Ops:
  0.6 0.0 copy-start.6
  0.6 0.6 %copy-done.6 = s32[4]{0:T(128)S(1)} copy-done((s32[4]{0:T(128)S(1)}, s32[4]{0:T(128)}, u32[]{:S(2)}) %copy-start.6) | copy-done | bytes 40
  1.3 0.0 copy-start
  1.3 1.0 %copy-done = bf16[5,5,8,8,128]{4,3,2,1,0:T(8,128)(2,1)S(1)} copy-done((bf16[5,5,8,8,128]{4,3,2,1,0:T(8,128)(2,1)S(1)}, bf16[5,5,8,8,128]{4,3,2,1,0:T(8,128)(2,1)}, u32[]{:S(2)}) %copy-start) | copy-done | bytes 409624
  2.3 0.0 copy-start.1
  2.3 1.0 %copy-done.1 = bf16[5,5,8,8,128]{4,3,2,1,0:T(8,128)(2,1)S(1)} copy-done((bf16[5,5,8,8,128]{4,3,2,1,0:T(8,128)(2,1)S(1)}, bf16[5,5,8,8,128]{4,3,2,1,0:T(8,128)(2,1)}, u32[]{:S(2)}) %copy-start.1) | copy-done | bytes 409624
  3.3 0.0 copy-start.2
  3.3 0.9 %copy-done.2 = f32[5,8,8,128]{3,2,1,0:T(8,128)S(1)} copy-done((f32[5,8,8,128]{3,2,1,0:T(8,128)S(1)}, f32[5,8,8,128]{3,2,1,0:T(8,128)}, u32[]{:S(2)}) %copy-start.2) | copy-done | bytes 163864
  4.2 0.0 copy-start.3
  4.2 0.9 %copy-done.3 = f32[5,8,8,128]{3,2,1,0:T(8,128)S(1)} copy-done((f32[5,8,8,128]{3,2,1,0:T(8,128)S(1)}, f32[5,8,8,128]{3,2,1,0:T(8,128)}, u32[]{:S(2)}) %copy-start.3) | copy-done | bytes 163864
  5.1 0.0 copy-start.4
  5.1 0.9 %copy-done.4 = f32[3,8,8,128]{3,2,1,0:T(8,128)S(1)} copy-done((f32[3,8,8,128]{3,2,1,0:T(8,128)S(1)}, f32[3,8,8,128]{3,2,1,0:T(8,128)}, u32[]{:S(2)}) %copy-start.4) | copy-done | bytes 98328
  6.0 0.0 copy-start.5
  6.0 0.8 %copy-done.5 = s32[8,8,128]{2,1,0:T(8,128)S(1)} copy-done((s32[8,8,128]{2,1,0:T(8,128)S(1)}, s32[8,8,128]{2,1,0:T(8,128)}, u32[]{:S(2)}) %copy-start.5) | copy-done | bytes 32792
  6.8 26.1 %shard_map.86 = (f32[320,128]{1,0:T(8,128)S(1)}, f32[5,16,128]{2,1,0:T(8,128)S(1)}) custom-call(s32[4]{0:T(128)S(1)} %copy-done.6, f32[320,128]{1,0:T(8,128)S(1)} %bitcast.10, f32[320,128]{1,0:T(8,128)S(1)} %bitcast.11, bf16[25,64,128]{2,1,0:T(8,128)(2,1)S(1)} %bitcast.8, bf16[25,64,128]{2,1,0:T(8,128)(2,1)S(1)} %bitcast.9, f32[192,128]{1,0:T(8,128)S(1)} %bitcast.13, ...), custom_call_target="tpu_custom_call" | custom-call | tf_op jit(solution)/shard_map/pallas_call | solution.py:311
  32.9 0.8 %reshape.35 = f32[1,5,16,4,16]{4,3,2,1,0:T(4,128)} reshape(f32[5,16,64]{2,1,0:T(8,128)S(1)} %bitcast.14) | data formatting | bytes 40960 | tf_op jit(solution)/shard_map/reshape | solution.py:356
  33.7 0.7 %copy.10 = f32[5,8,8,128]{3,2,1,0:T(8,128)} copy(f32[5,8,8,128]{3,2,1,0:T(8,128)S(1)} %bitcast.12) | data formatting | bytes 327680
Async XLA Ops:
  0.6 0.7 %copy-start.6 = (s32[4]{0:T(128)S(1)}, s32[4]{0:T(128)}, u32[]{:S(2)}) copy-start(s32[4]{0:T(128)} %owner.1) | copy-start | bytes 52
  1.3 1.0 %copy-start = (bf16[5,5,8,8,128]{4,3,2,1,0:T(8,128)(2,1)S(1)}, bf16[5,5,8,8,128]{4,3,2,1,0:T(8,128)(2,1)}, u32[]{:S(2)}) copy-start(bf16[5,5,8,8,128]{4,3,2,1,0:T(8,128)(2,1)} %param.9) | copy-start | bytes 1228804
  2.3 1.0 %copy-start.1 = (bf16[5,5,8,8,128]{4,3,2,1,0:T(8,128)(2,1)S(1)}, bf16[5,5,8,8,128]{4,3,2,1,0:T(8,128)(2,1)}, u32[]{:S(2)}) copy-start(bf16[5,5,8,8,128]{4,3,2,1,0:T(8,128)(2,1)} %param.10) | copy-start | bytes 1228804
  3.3 0.9 %copy-start.2 = (f32[5,8,8,128]{3,2,1,0:T(8,128)S(1)}, f32[5,8,8,128]{3,2,1,0:T(8,128)}, u32[]{:S(2)}) copy-start(f32[5,8,8,128]{3,2,1,0:T(8,128)} %param.7) | copy-start | bytes 491524
  4.2 0.9 %copy-start.3 = (f32[5,8,8,128]{3,2,1,0:T(8,128)S(1)}, f32[5,8,8,128]{3,2,1,0:T(8,128)}, u32[]{:S(2)}) copy-start(f32[5,8,8,128]{3,2,1,0:T(8,128)} %param.8) | copy-start | bytes 491524
  5.1 0.9 %copy-start.4 = (f32[3,8,8,128]{3,2,1,0:T(8,128)S(1)}, f32[3,8,8,128]{3,2,1,0:T(8,128)}, u32[]{:S(2)}) copy-start(f32[3,8,8,128]{3,2,1,0:T(8,128)} %param.11) | copy-start | bytes 294916
  6.0 0.8 %copy-start.5 = (s32[8,8,128]{2,1,0:T(8,128)S(1)}, s32[8,8,128]{2,1,0:T(8,128)}, u32[]{:S(2)}) copy-start(s32[8,8,128]{2,1,0:T(8,128)} %param.12) | copy-start | bytes 98308
where the time goes:
time: 34.7 us; the launch traced here: 34.3 us
  Pallas kernels  26.1 us (75%)
  local copies, waits for them, and re-layouts  7.6 us (22%)
  between operations  0.66 us (2%)
    pallas_call x1, Pallas kernels, shards(): pl.pallas_call(functools.partial(kernel, bricks, levels, fields, nx, ny,...  26.1 us
    unnamed x15, local copies, waits for them, and re-layouts  6.8 us
    reshape x1, local copies, waits for them, and re-layouts, shards(): coarse[:, :, :half_y * zblock]  0.8 us

commit v1 on v0

--- a/solution.py
+++ b/solution.py
@@ -14,16 +14,17 @@
 
 def kernel(
     bricks, levels, fields, nx, ny, zblock,
-    owner, adjoint, source, block, precond, couple, solid,
+    owners, adjoint, source, block, precond, couple, solid,
     smoothed, coarse,
-    cells, src, raw_b, raw_p, mat_b, mat_p, cpl, sld, near, part, out_halo, in_halo,
-    rows_x, packed, got, got_edge, merged,
+    owner, cells, src, raw_b, raw_p, mat_b, mat_p, cpl, sld, near, part, out_halo, in_halo,
+    beyond, rows_x, rows_b, packed, got, got_edge, got_low, merged,
     in_sem, out_sem, halo_send, halo_recv, end_send, end_recv,
 ):
     plane = nx * ny
     nz = cells.shape[1]
     half_x, half_y = nx // 2, ny // 2
-    width = half_x + 1
+    width = half_x + 2
+    halo = fields * max(nx, ny)
     pad = rows_x.shape[0] // ny
     b, l = lax.axis_index("brick"), lax.axis_index("level")
     has = (l < levels - 1, l > 0, b < bricks - 1, b > 0)
@@ -35,7 +36,7 @@
         for i, (a, v) in enumerate(
             (
                 (adjoint, cells), (couple, cpl), (block, raw_b),
-                (source, src), (solid, sld), (precond, raw_p),
+                (source, src), (solid, sld), (precond, raw_p), (owners, owner),
             )
         )
     ]
@@ -60,17 +61,22 @@
 
         @pl.when(jnp.logical_not(has[i]))
         def _():
-            for e in range(SWEEPS + 1):
+            for e in range(SWEEPS):
                 in_halo[e, i] = jnp.zeros(in_halo.shape[2:], jnp.float32)
 
     @pl.when(jnp.logical_not(has[3]))
     def _():
         got_edge[...] = jnp.zeros_like(got_edge)
 
+    @pl.when(jnp.logical_not(has[2]))
+    def _():
+        got_low[...] = jnp.zeros_like(got_low)
+
     def halo_copy(e, i):
+        rows = pl.ds(0, out_halo.shape[2] if e == 1 else halo)
         return pltpu.make_async_remote_copy(
-            src_ref=out_halo.at[e, i],
-            dst_ref=in_halo.at[e, i],
+            src_ref=out_halo.at[e, i, rows],
+            dst_ref=in_halo.at[e, i, rows],
             send_sem=halo_send.at[e, i],
             recv_sem=halo_recv.at[e, i],
             device_id=dest[i],
@@ -85,6 +91,21 @@
             to = f * ny
             out_halo[e, 0, to : to + ny] = cells[at : at + ny]
             out_halo[e, 1, to : to + ny] = cells[at + plane - ny : at + plane]
+        if e == 1:
+            edges = (
+                (0, slice(0, ny), 0, ny),
+                (1, slice(plane - ny, plane), 0, ny),
+                (2, pl.ds(0, nx, stride=ny), plane, nx),
+                (3, pl.ds(ny - 1, nx, stride=ny), plane, nx),
+            )
+            for i, spot, at, count in edges:
+                if i < 2:
+                    open_cells = sld[spot] == 0
+                    weights = cpl[spot]
+                else:
+                    open_cells = sld[spot, :] == 0
+                    weights = cpl[pl.ds(at + (ny - 1 if i == 3 else 0), nx, stride=ny), :]
+                out_halo[e, i, halo : halo + count] = jnp.where(open_cells, weights, 0.0)
         for i in (2, 3, 0, 1):
 
             @pl.when(can_send[i])
@@ -157,6 +178,7 @@
         local_part(f)
     loads[4].wait()
     loads[5].wait()
+    loads[6].wait()
     keep = sld[...] == 0
     for i in range(fields * fields):
         mat_p[i] = jnp.where(keep, RELAX * raw_p[i].astype(jnp.float32), 0.0)
@@ -174,7 +196,8 @@
             for g in range(fields):
                 total = total + mat_p[f * fields + g] * part[g * plane : (g + 1) * plane]
             cells[at : at + plane] = total
-        send(sweep + 1)
+        if sweep < SWEEPS - 1:
+            send(sweep + 1)
 
     store = pltpu.make_async_copy(cells, smoothed, out_sem)
     store.start()
@@ -191,28 +214,45 @@
         gap == 0, 0.5, jnp.where((gap == 1) | (gap == -1), 0.25, 0.0)
     ).astype(jnp.bfloat16)
     rows_x[...] = jnp.zeros_like(rows_x)
-    arrive(SWEEPS)
+    rows_b[...] = jnp.zeros_like(rows_b)
+    beyond[...] = jnp.zeros_like(beyond)
+    high_x, low_x = (in_halo[1, i, halo : halo + ny] for i in (0, 1))
+    high_y, low_y = (in_halo[1, i, halo : halo + nx] for i in (2, 3))
+
+    def restrict_x(target, f, cut):
+        for k in range(-1, half_x + 1):
+            value = 0.0
+            for x, factor in ((2 * k - 1, 0.25), (2 * k, 0.5), (2 * k + 1, 0.25)):
+                if x in cut:
+                    value = value + factor * cut[x]
+            if k >= 0 or -1 in cut:
+                spot = (f * width + k + 1) * ny
+                target[spot : spot + ny] = value
 
     for f in range(fields):
         res = jnp.where(keep, part[f * plane : (f + 1) * plane], 0.0)
-        cut = [res[x * ny : (x + 1) * ny] for x in range(nx)]
-        for k in range(width):
-            if k == half_x:
-                value = 0.25 * cut[nx - 1]
-            else:
-                value = 0.5 * cut[2 * k] + 0.25 * cut[2 * k + 1]
-                if k:
-                    value = value + 0.25 * cut[2 * k - 1]
-            spot = (f * width + k) * ny
-            rows_x[spot : spot + ny] = value
-    line = [rows_x[pl.ds(y, pad, stride=ny), :] for y in range(ny)]
+        cut = {x: res[x * ny : (x + 1) * ny] for x in range(nx)}
+        at = f * plane
+        cut[-1] = low_x * cells[at : at + ny]
+        cut[nx] = high_x * cells[at + plane - ny : at + plane]
+        restrict_x(rows_x, f, cut)
+        beyond[pl.ds(at, nx, stride=ny), :] = low_y * cells[pl.ds(at, nx, stride=ny), :]
+        beyond[pl.ds(at + 1, nx, stride=ny), :] = (
+            high_y * cells[pl.ds(at + ny - 1, nx, stride=ny), :]
+        )
+        restrict_x(
+            rows_b, f, {x: beyond[at + x * ny : at + (x + 1) * ny] for x in range(nx)}
+        )
+    line = {y: rows_x[pl.ds(y, pad, stride=ny), :] for y in range(ny)}
+    line[-1] = rows_b[pl.ds(0, pad, stride=ny), :]
+    line[ny] = rows_b[pl.ds(1, pad, stride=ny), :]
     groups = []
-    for k in range(half_y):
-        value = 0.5 * line[2 * k] + 0.25 * line[2 * k + 1]
-        if k:
-            value = value + 0.25 * line[2 * k - 1]
+    for k in [*range(half_y + 1), -1]:
+        value = 0.0
+        for y, factor in ((2 * k - 1, 0.25), (2 * k, 0.5), (2 * k + 1, 0.25)):
+            if y in line:
+                value = value + factor * line[y]
         groups.append(value)
-    groups.append(0.25 * line[ny - 1])
     stacked = jnp.concatenate(groups, 0)
     high = stacked.astype(jnp.bfloat16)
     low = (stacked - high.astype(jnp.float32)).astype(jnp.bfloat16)
@@ -222,7 +262,7 @@
     spot_of = lax.broadcasted_iota(jnp.int32, (pad, nz), 1) // zblock
     for d in range(levels):
         total = jnp.zeros((pad, nz), jnp.float32)
-        for k in range(half_y + 1):
+        for k in range(half_y + 2):
             shift = ((k - d) * zblock) % nz
             moved = product[k * pad : (k + 1) * pad]
             if shift:
@@ -234,10 +274,10 @@
         to = lax.rem(l + k, levels)
         return pltpu.make_async_remote_copy(
             src_ref=packed.at[to],
-            dst_ref=(got_edge if edge else got).at[l],
+            dst_ref=(got, got_edge, got_low)[edge].at[l],
             send_sem=end_send.at[edge, k],
             recv_sem=end_recv.at[edge, k],
-            device_id=(b + edge, to),
+            device_id=(b + (0, 1, -1)[edge], to),
             device_id_type=MESH,
         )
 
@@ -245,7 +285,7 @@
         origin = lax.rem(l + levels - k, levels)
         return pltpu.make_async_remote_copy(
             src_ref=packed.at[l],
-            dst_ref=(got_edge if edge else got).at[origin],
+            dst_ref=(got, got_edge, got_low)[edge].at[origin],
             send_sem=end_send.at[edge, k],
             recv_sem=end_recv.at[edge, k],
             device_id=(b, origin),
@@ -257,11 +297,16 @@
         for k in range(levels):
             end_copy(k, 1).start()
 
+    @pl.when(has[3])
+    def _():
+        for k in range(levels):
+            end_copy(k, 2).start()
+
     for k in range(1, levels):
         end_copy(k, 0).start()
     got[l] = packed[l]
     store.wait()
-    for e in range(SWEEPS + 1):
+    for e in range(SWEEPS):
         for i in range(4):
 
             @pl.when(can_send[i])
@@ -276,17 +321,28 @@
         for k in range(levels):
             end_arrival(k, 1).wait_recv()
 
+    @pl.when(has[2])
+    def _():
+        for k in range(levels):
+            end_arrival(k, 2).wait_recv()
+
     for s in range(levels):
-        edge = pltpu.roll(got_edge[s], (-half_y * zblock) % nz, 1)
-        merged[s] = got[s] + jnp.where(spot_of == 0, edge, 0.0)
+        after = pltpu.roll(got_edge[s], (-half_y * zblock) % nz, 1)
+        before = pltpu.roll(got_low[s], (-2 * zblock) % nz, 1)
+        merged[s] = (
+            got[s]
+            + jnp.where(spot_of == 0, after, 0.0)
+            + jnp.where(spot_of == half_y - 1, before, 0.0)
+        )
     for f in range(fields):
+        at = f * width
         for s in range(levels):
-            at = f * width
-            coarse[f, s * half_x : (s + 1) * half_x] = merged[s, at : at + half_x]
-            if s:
-                coarse[f, s * half_x : s * half_x + 1] = (
-                    merged[s, at : at + 1] + merged[s - 1, at + half_x : at + width]
-                )
+            to = s * half_x
+            coarse[f, to : to + half_x] = merged[s, at + 1 : at + 1 + half_x]
+        for s in range(1, levels):
+            to = s * half_x
+            coarse[f, to : to + 1] += merged[s - 1, at + width - 1 : at + width]
+            coarse[f, to - 1 : to] += merged[s, at : at + 1]
 
     for k in range(1, levels):
         end_copy(k, 0).wait_send()
@@ -295,6 +351,11 @@
     def _():
         for k in range(levels):
             end_copy(k, 1).wait_send()
+
+    @pl.when(has[3])
+    def _():
+        for k in range(levels):
+            end_copy(k, 2).wait_send()
 
 
 def shards(bricks, levels, adjoint, source, block, precond, couple, solid, coarse_owner):
@@ -302,21 +363,22 @@
     plane = nx * ny
     zblock = nz // (2 * levels)
     half_x, half_y = nx // 2, ny // 2
-    pad = -(-fields * (half_x + 1) // 8) * 8
+    pad = -(-fields * (half_x + 2) // 8) * 8
     flat = fields * plane
     halo = fields * max(nx, ny)
     f32, bf16 = jnp.float32, jnp.bfloat16
     vmem, dma = pltpu.VMEM, pltpu.SemaphoreType.DMA
-    anywhere = pl.BlockSpec(memory_space=pl.ANY)
+    anywhere = pl.BlockSpec(memory_space=pltpu.HBM)
     cells, coarse = pl.pallas_call(
         functools.partial(kernel, bricks, levels, fields, nx, ny, zblock),
         out_shape=(
             jax.ShapeDtypeStruct((flat, nz), f32),
             jax.ShapeDtypeStruct((fields, levels * half_x, nz), f32),
         ),
-        in_specs=[pl.BlockSpec(memory_space=pltpu.SMEM)] + [anywhere] * 6,
+        in_specs=[anywhere] * 7,
         out_specs=(anywhere, pl.BlockSpec(memory_space=pltpu.VMEM)),
         scratch_shapes=[
+            pltpu.SMEM((levels,), jnp.int32),
             vmem((flat, nz), f32),
             vmem((flat, nz), f32),
             vmem((fields * fields, plane, nz), bf16),
@@ -327,22 +389,25 @@
             vmem((plane, nz), jnp.int32),
             vmem((4, plane, nz), f32),
             vmem((flat, nz), f32),
-            vmem((SWEEPS + 1, 4, halo, nz), f32),
-            vmem((SWEEPS + 1, 4, halo, nz), f32),
+            vmem((SWEEPS, 4, halo + max(nx, ny), nz), f32),
+            vmem((SWEEPS, 4, halo + max(nx, ny), nz), f32),
+            vmem((flat, nz), f32),
+            vmem((pad * ny, nz), f32),
             vmem((pad * ny, nz), f32),
             vmem((levels, pad, nz), f32),
             vmem((levels, pad, nz), f32),
             vmem((levels, pad, nz), f32),
             vmem((levels, pad, nz), f32),
-            dma((6,)),
+            vmem((levels, pad, nz), f32),
+            dma((7,)),
             dma,
-            dma((SWEEPS + 1, 4)),
-            dma((SWEEPS + 1, 4)),
-            dma((2, levels)),
-            dma((2, levels)),
+            dma((SWEEPS, 4)),
+            dma((SWEEPS, 4)),
+            dma((3, levels)),
+            dma((3, levels)),
         ],
         compiler_params=pltpu.CompilerParams(
-            collective_id=0, has_side_effects=True, vmem_limit_bytes=32 * 1024 * 1024
+            collective_id=0, has_side_effects=True, vmem_limit_bytes=60 * 1024 * 1024
         ),
     )(
         coarse_owner,

time: 34.7 us -> 26.3 us (0.76)
  local copies, waits for them, and re-layouts: 7.6 us -> 2.28 us
  Pallas kernels: 26.1 us -> 23.2 us
    unnamed x15 -> x3, local copies, waits for them, and re-layouts: 6.8 us -> 0.67 us
    pallas_call x1, Pallas kernels: 26.1 us -> 23.2 us  [shards(): pl.pallas_call(functools.partial(kernel, bricks, levels, fields, nx, ny,...]
    reshape x1, local copies, waits for them, and re-layouts: 0.8 us -> 1.61 us  [shards(): coarse[:, :, :half_y * zblock]]
where the time goes in v1:
time: 26.3 us; the launch traced here: 26.2 us
  Pallas kernels  23.2 us (88%)
  local copies, waits for them, and re-layouts  2.28 us (9%)
  between operations  0.65 us (2%)
    pallas_call x1, Pallas kernels, shards(): pl.pallas_call(functools.partial(kernel, bricks, levels, fields, nx, ny,...  23.2 us
    reshape x1, local copies, waits for them, and re-layouts, shards(): coarse[:, :, :half_y * zblock]  1.61 us
    unnamed x3, local copies, waits for them, and re-layouts  0.67 us

profile of v1, /device:TPU:0, one launch (start us, length us, event | category | flops | bytes accessed | tf_op | source)
XLA Modules:
  0.0 26.2 jit_solution(2697165446468060104)
XLA Ops:
  0.6 23.2 %shard_map.86 = (f32[320,128]{1,0:T(8,128)}, f32[5,16,128]{2,1,0:T(8,128)}) custom-call(s32[4]{0:T(128)} %owners.1, f32[320,128]{1,0:T(8,128)} %bitcast.10, f32[320,128]{1,0:T(8,128)} %bitcast.11, bf16[25,64,128]{2,1,0:T(8,128)(2,1)} %bitcast.8, bf16[25,64,128]{2,1,0:T(8,128)(2,1)} %bitcast.9, f32[192,128]{1,0:T(8,128)} %bitcast.13, s32[64,128]{1,0:T(8,128)} %bitcast.15), custom_call_target="tpu_custom_call" | custom-call | tf_op jit(solution)/shard_map/pallas_call | solution.py:372
  23.9 0.0 copy-start
  23.9 1.6 %reshape.35 = f32[1,5,16,4,16]{4,3,2,1,0:T(4,128)} reshape(f32[5,16,64]{2,1,0:T(8,128)} %bitcast.14) | data formatting | bytes 40960 | tf_op jit(solution)/shard_map/reshape | solution.py:421
  25.5 0.0 copy-done
  25.5 0.7 %copy.10 = f32[5,8,8,128]{3,2,1,0:T(8,128)} copy(f32[5,8,8,128]{3,2,1,0:T(8,128)S(1)} %bitcast.12) | data formatting | bytes 327680
Async XLA Ops:
  23.9 1.6 %copy-start = (f32[320,128]{1,0:T(8,128)S(1)}, f32[320,128]{1,0:T(8,128)}, u32[]{:S(2)}) copy-start(f32[320,128]{1,0:T(8,128)} %get-tuple-element.4) | copy-start | bytes 491524

commit v2 on v1

--- a/solution.py
+++ b/solution.py
@@ -17,7 +17,7 @@
     owners, adjoint, source, block, precond, couple, solid,
     smoothed, coarse,
     owner, cells, src, raw_b, raw_p, mat_b, mat_p, cpl, sld, near, part, out_halo, in_halo,
-    beyond, rows_x, rows_b, packed, got, got_edge, got_low, merged,
+    beyond, rows_x, rows_b, packed, packed_edge, sides, got, got_edge, got_low, merged,
     in_sem, out_sem, halo_send, halo_recv, end_send, end_recv,
 ):
     plane = nx * ny
@@ -83,14 +83,12 @@
             device_id_type=MESH,
         )
 
+    def start(e, i):
+        @pl.when(can_send[i])
+        def _():
+            halo_copy(e, i).start()
+
     def send(e):
-        for f in range(fields):
-            at, to = f * plane, f * nx
-            out_halo[e, 2, to : to + nx] = cells[pl.ds(at, nx, stride=ny), :]
-            out_halo[e, 3, to : to + nx] = cells[pl.ds(at + ny - 1, nx, stride=ny), :]
-            to = f * ny
-            out_halo[e, 0, to : to + ny] = cells[at : at + ny]
-            out_halo[e, 1, to : to + ny] = cells[at + plane - ny : at + plane]
         if e == 1:
             edges = (
                 (0, slice(0, ny), 0, ny),
@@ -106,11 +104,19 @@
                     open_cells = sld[spot, :] == 0
                     weights = cpl[pl.ds(at + (ny - 1 if i == 3 else 0), nx, stride=ny), :]
                 out_halo[e, i, halo : halo + count] = jnp.where(open_cells, weights, 0.0)
-        for i in (2, 3, 0, 1):
-
-            @pl.when(can_send[i])
-            def _():
-                halo_copy(e, i).start()
+        if e == 0:
+            for f in range(fields):
+                at, to = f * plane, f * nx
+                out_halo[e, 2, to : to + nx] = cells[pl.ds(at, nx, stride=ny), :]
+                out_halo[e, 3, to : to + nx] = cells[pl.ds(at + ny - 1, nx, stride=ny), :]
+        start(e, 2)
+        start(e, 3)
+        for f in range(fields):
+            at, to = f * plane, f * ny
+            out_halo[e, 0, to : to + ny] = cells[at : at + ny]
+            out_halo[e, 1, to : to + ny] = cells[at + plane - ny : at + plane]
+        start(e, 0)
+        start(e, 1)
 
     loads[0].wait()
     neighbours = (levels - 1) + levels * (
@@ -153,26 +159,37 @@
             total[plane - ny :] + c[plane - ny :] * mid[plane - 2 * ny : plane - ny]
         )
 
-    def arrive(e):
-        for i in (2, 3, 0, 1):
-
-            @pl.when(has[i])
-            def _():
-                halo_copy(e, i).wait_recv()
-
-        low_y = cpl[pl.ds(plane, nx, stride=ny), :]
-        high_y = cpl[pl.ds(plane + ny - 1, nx, stride=ny), :]
-        low_x, high_x = cpl[0:ny], cpl[plane - ny : plane]
+    def arrive(e, i):
+        @pl.when(has[i])
+        def _():
+            halo_copy(e, i).wait_recv()
+
+    def add_x(e):
+        arrive(e, 0)
+        arrive(e, 1)
         for f in range(fields):
             at = f * plane
             mine = slice(f * ny, (f + 1) * ny)
-            part[at + plane - ny : at + plane] += high_x * in_halo[e, 0, mine]
-            part[at : at + ny] += low_x * in_halo[e, 1, mine]
-            mine = slice(f * nx, (f + 1) * nx)
-            spot = pl.ds(at + ny - 1, nx, stride=ny)
-            part[spot, :] = part[spot, :] + high_y * in_halo[e, 2, mine]
-            spot = pl.ds(at, nx, stride=ny)
-            part[spot, :] = part[spot, :] + low_y * in_halo[e, 3, mine]
+            spot = slice(at + plane - ny, at + plane)
+            part[spot] += cpl[plane - ny : plane] * in_halo[e, 0, mine]
+            part[at : at + ny] += cpl[0:ny] * in_halo[e, 1, mine]
+
+    def add_y(e):
+        for i in (2, 3):
+            arrive(e, i)
+            row_at = ny - 1 if i == 2 else 0
+            weights = cpl[pl.ds(plane + row_at, nx, stride=ny), :]
+            change = [
+                weights * in_halo[e, i, g * nx : (g + 1) * nx] for g in range(fields)
+            ]
+            for f in range(fields):
+                spot = pl.ds(f * plane + row_at, nx, stride=ny)
+                total = cells[spot, :]
+                for g in range(fields):
+                    total = total + sides[i - 2, f * fields + g] * change[g]
+                cells[spot, :] = total
+                if e < SWEEPS - 1:
+                    out_halo[e + 1, 5 - i, f * nx : (f + 1) * nx] = total
 
     for f in range(fields):
         local_part(f)
@@ -182,12 +199,14 @@
     keep = sld[...] == 0
     for i in range(fields * fields):
         mat_p[i] = jnp.where(keep, RELAX * raw_p[i].astype(jnp.float32), 0.0)
+        sides[0, i] = mat_p[i, pl.ds(ny - 1, nx, stride=ny), :]
+        sides[1, i] = mat_p[i, pl.ds(0, nx, stride=ny), :]
 
     for sweep in range(SWEEPS):
         if sweep:
             for f in range(fields):
                 local_part(f)
-        arrive(sweep)
+        add_x(sweep)
         for f in range(fields):
             at = f * plane
             total = cells[at : at + plane]
@@ -196,6 +215,7 @@
             for g in range(fields):
                 total = total + mat_p[f * fields + g] * part[g * plane : (g + 1) * plane]
             cells[at : at + plane] = total
+        add_y(sweep)
         if sweep < SWEEPS - 1:
             send(sweep + 1)
 
@@ -262,18 +282,28 @@
     spot_of = lax.broadcasted_iota(jnp.int32, (pad, nz), 1) // zblock
     for d in range(levels):
         total = jnp.zeros((pad, nz), jnp.float32)
-        for k in range(half_y + 2):
+        for k in range(half_y):
             shift = ((k - d) * zblock) % nz
             moved = product[k * pad : (k + 1) * pad]
             if shift:
                 moved = pltpu.roll(moved, shift, 1)
             total = jnp.where(spot_of == k, moved, total)
         packed[d] = total
+        for side in range(2):
+            total = jnp.zeros((8, nz), jnp.float32)
+            for k in range(pad // 8):
+                at = (half_y + side) * pad + k * 8
+                moved = product[at : at + 8]
+                shift = ((k - d) * zblock) % nz
+                if shift:
+                    moved = pltpu.roll(moved, shift, 1)
+                total = jnp.where(spot_of[:8] == k, moved, total)
+            packed_edge[side, d] = total
 
     def end_copy(k, edge):
         to = lax.rem(l + k, levels)
         return pltpu.make_async_remote_copy(
-            src_ref=packed.at[to],
+            src_ref=packed_edge.at[edge - 1, to] if edge else packed.at[to],
             dst_ref=(got, got_edge, got_low)[edge].at[l],
             send_sem=end_send.at[edge, k],
             recv_sem=end_recv.at[edge, k],
@@ -284,7 +314,7 @@
     def end_arrival(k, edge):
         origin = lax.rem(l + levels - k, levels)
         return pltpu.make_async_remote_copy(
-            src_ref=packed.at[l],
+            src_ref=packed_edge.at[edge - 1, l] if edge else packed.at[l],
             dst_ref=(got, got_edge, got_low)[edge].at[origin],
             send_sem=end_send.at[edge, k],
             recv_sem=end_recv.at[edge, k],
@@ -327,13 +357,15 @@
             end_arrival(k, 2).wait_recv()
 
     for s in range(levels):
-        after = pltpu.roll(got_edge[s], (-half_y * zblock) % nz, 1)
-        before = pltpu.roll(got_low[s], (-2 * zblock) % nz, 1)
-        merged[s] = (
-            got[s]
-            + jnp.where(spot_of == 0, after, 0.0)
-            + jnp.where(spot_of == half_y - 1, before, 0.0)
-        )
+        for k in range(pad // 8):
+            first = pltpu.roll(got_edge[s], (-k * zblock) % nz, 1)
+            last = pltpu.roll(got_low[s], ((half_y - 1 - k) * zblock) % nz, 1)
+            mine = slice(k * 8, k * 8 + 8)
+            merged[s, mine] = (
+                got[s, mine]
+                + jnp.where(spot_of[:8] == 0, first, 0.0)
+                + jnp.where(spot_of[:8] == half_y - 1, last, 0.0)
+            )
     for f in range(fields):
         at = f * width
         for s in range(levels):
@@ -395,9 +427,11 @@
             vmem((pad * ny, nz), f32),
             vmem((pad * ny, nz), f32),
             vmem((levels, pad, nz), f32),
+            vmem((2, levels, 8, nz), f32),
+            vmem((2, fields * fields, nx, nz), f32),
             vmem((levels, pad, nz), f32),
-            vmem((levels, pad, nz), f32),
-            vmem((levels, pad, nz), f32),
+            vmem((levels, 8, nz), f32),
+            vmem((levels, 8, nz), f32),
             vmem((levels, pad, nz), f32),
             dma((7,)),
             dma,

time: 26.3 us -> 25.6 us (0.973)
  Pallas kernels: 23.2 us -> 22.5 us
    pallas_call x1, Pallas kernels: 23.2 us -> 22.5 us  [shards(): pl.pallas_call(functools.partial(kernel, bricks, levels, fields, nx, ny,...]
where the time goes in v2:
time: 25.6 us; the launch traced here: 25.4 us
  Pallas kernels  22.5 us (88%)
  local copies, waits for them, and re-layouts  2.28 us (9%)
  between operations  0.65 us (3%)
    pallas_call x1, Pallas kernels, shards(): pl.pallas_call(functools.partial(kernel, bricks, levels, fields, nx, ny,...  22.5 us
    reshape x1, local copies, waits for them, and re-layouts, shards(): coarse[:, :, :half_y * zblock]  1.61 us
    unnamed x3, local copies, waits for them, and re-layouts  0.67 us

profile of v2, /device:TPU:0, one launch (start us, length us, event | category | flops | bytes accessed | tf_op | source)
XLA Modules:
  0.0 25.4 jit_solution(4805931703393836568)
XLA Ops:
  0.6 22.5 %shard_map.86 = (f32[320,128]{1,0:T(8,128)}, f32[5,16,128]{2,1,0:T(8,128)}) custom-call(s32[4]{0:T(128)} %owners.1, f32[320,128]{1,0:T(8,128)} %bitcast.10, f32[320,128]{1,0:T(8,128)} %bitcast.11, bf16[25,64,128]{2,1,0:T(8,128)(2,1)} %bitcast.8, bf16[25,64,128]{2,1,0:T(8,128)(2,1)} %bitcast.9, f32[192,128]{1,0:T(8,128)} %bitcast.13, s32[64,128]{1,0:T(8,128)} %bitcast.15), custom_call_target="tpu_custom_call" | custom-call | tf_op jit(solution)/shard_map/pallas_call | solution.py:404
  23.1 0.0 copy-start
  23.2 1.6 %reshape.35 = f32[1,5,16,4,16]{4,3,2,1,0:T(4,128)} reshape(f32[5,16,64]{2,1,0:T(8,128)} %bitcast.14) | data formatting | bytes 40960 | tf_op jit(solution)/shard_map/reshape | solution.py:455
  24.8 0.0 copy-done
  24.8 0.7 %copy.10 = f32[5,8,8,128]{3,2,1,0:T(8,128)} copy(f32[5,8,8,128]{3,2,1,0:T(8,128)S(1)} %bitcast.12) | data formatting | bytes 327680
Async XLA Ops:
  23.1 1.6 %copy-start = (f32[320,128]{1,0:T(8,128)S(1)}, f32[320,128]{1,0:T(8,128)}, u32[]{:S(2)}) copy-start(f32[320,128]{1,0:T(8,128)} %get-tuple-element.4) | copy-start | bytes 491524

commit v3 on v2

--- a/solution.py
+++ b/solution.py
@@ -405,7 +405,7 @@
         functools.partial(kernel, bricks, levels, fields, nx, ny, zblock),
         out_shape=(
             jax.ShapeDtypeStruct((flat, nz), f32),
-            jax.ShapeDtypeStruct((fields, levels * half_x, nz), f32),
+            vmem((fields, levels * half_x, nz), f32),
         ),
         in_specs=[anywhere] * 7,
         out_specs=(anywhere, pl.BlockSpec(memory_space=pltpu.VMEM)),

time: 25.6 us -> 24.3 us (0.949)
  local copies, waits for them, and re-layouts: 2.28 us -> 1.57 us
  Pallas kernels: 22.5 us -> 21.9 us
    reshape x1, local copies, waits for them, and re-layouts: 1.61 us -> 0.8 us  [shards(): coarse[:, :, :half_y * zblock]]
    pallas_call x1, Pallas kernels: 22.5 us -> 21.9 us  [shards(): pl.pallas_call(functools.partial(kernel, bricks, levels, fields, nx, ny,...]
where the time goes in v3:
time: 24.3 us; the launch traced here: 24.1 us
  Pallas kernels  21.9 us (90%)
  local copies, waits for them, and re-layouts  1.57 us (6%)
  between operations  0.65 us (3%)
    pallas_call x1, Pallas kernels, shards(): pl.pallas_call(functools.partial(kernel, bricks, levels, fields, nx, ny,...  21.9 us
    reshape x1, local copies, waits for them, and re-layouts, shards(): coarse[:, :, :half_y * zblock]  0.8 us
    unnamed x3, local copies, waits for them, and re-layouts  0.77 us

profile of v3, /device:TPU:0, one launch (start us, length us, event | category | flops | bytes accessed | tf_op | source)
XLA Modules:
  0.0 24.1 jit_solution(14193074907183849050)
XLA Ops:
  0.6 21.9 %shard_map.86 = (f32[320,128]{1,0:T(8,128)}, f32[5,16,128]{2,1,0:T(8,128)S(1)}) custom-call(s32[4]{0:T(128)} %owners.1, f32[320,128]{1,0:T(8,128)} %bitcast.11, f32[320,128]{1,0:T(8,128)} %bitcast.12, bf16[25,64,128]{2,1,0:T(8,128)(2,1)} %bitcast.9, bf16[25,64,128]{2,1,0:T(8,128)(2,1)} %bitcast.10, f32[192,128]{1,0:T(8,128)} %bitcast.14, s32[64,128]{1,0:T(8,128)} %bitcast.15), custom_call_target="tpu_custom_call" | custom-call | tf_op jit(solution)/shard_map/pallas_call | solution.py:404
  22.5 0.0 copy-start
  22.5 0.8 %reshape.35 = f32[1,5,16,4,16]{4,3,2,1,0:T(4,128)} reshape(f32[5,16,64]{2,1,0:T(8,128)S(1)} %bitcast.8) | data formatting | bytes 40960 | tf_op jit(solution)/shard_map/reshape | solution.py:455
  23.3 0.1 copy-done
  23.5 0.7 %copy.10 = f32[5,8,8,128]{3,2,1,0:T(8,128)} copy(f32[5,8,8,128]{3,2,1,0:T(8,128)S(1)} %bitcast.13) | data formatting | bytes 327680
Async XLA Ops:
  22.5 0.9 %copy-start = (f32[320,128]{1,0:T(8,128)S(1)}, f32[320,128]{1,0:T(8,128)}, u32[]{:S(2)}) copy-start(f32[320,128]{1,0:T(8,128)} %get-tuple-element.4) | copy-start | bytes 491524
